TPU v7x, 32 devices: a whole 2x2x4 slice. The times are simulated.
32 devices in a mesh: seq: 16 (over z, x, core), chan: 2 (over y).
Axes of the slice: x: 2, y: 2, z: 4, core: 2. Of those that a mesh axis runs over, the one named last changes fastest.
Arguments:
- loaded: bfloat16 [3, 16384, 4096], P(None, 'seq', 'chan'), may hold values from -6 to 6
- dest_tiles: int32 [512], P('seq'), may hold values from 0 to 255, as said below
- tile_counts: int32 [16], P('seq'), may hold values from 8 to 32, as said below
- segments: int32 [8192], P('seq'), may hold values from 0 to 31, never falling along the last dimension, each value on 1 to 1024 neighbouring positions
- short_filters: float32 [3, 7, 4096], P(None, None, 'chan')
- long_filters: bfloat16 [256, 8192], P('chan', 'seq')
- skip_gain: float32 [4096], P('chan'), may hold values from 0.5 to 1.5
- norm_gain: float32 [4096], P('chan'), may hold values from 0.5 to 1.5
Outputs:
- layer_out: bfloat16 [8192, 4096], P('seq', 'chan')
Inputs may be any that keep to these rules, and one draw needn't show every extreme that they name: Index s of seq holds tile_counts[s] tiles in its first slots; the busiest holds exactly 32, and every count is a multiple of 4. `dest_tiles`: entry s * 32 + j names the tile held in slot j of index s when j < tile_counts[s]; later slots name arbitrary tiles. The used slots name every tile exactly once. Tile d belongs to index d // 16 of seq, and one index holds either none or exactly 4 tiles of any one index.
All inputs are finite; a program needn't handle non-finite values.
Results may differ from a plain program's by a relative error of at most 0.0057.
Values may be sent and summed in bfloat16 or wider, within the bound.
A program may use at most 192 MiB of HBM per device.

v0:
```python
import math

import jax
import jax.numpy as jnp
from jax import lax
from jax.sharding import PartitionSpec as P

CHANNELS = 4096
TILES_DEV = 16


highest = lax.Precision.HIGHEST


def from_behind(block, axis, distance):
    devices = range(lax.axis_size(axis))
    route = [(i - distance, i) for i in devices if i - distance in devices]
    return lax.ppermute(block, axis, route)


def contract(einsum_form, left_side, right_side):
    return jnp.einsum(einsum_form, left_side, right_side, precision=highest)


def angles(first, second, period):
    turn_count = first[:, None] * second[None, :] % period
    return 2.0 * math.pi / period * turn_count.astype(jnp.float32)


def complex_apply(einsum_form, table_re, table_im, value_re, value_im):
    out_re = contract(einsum_form, table_re, value_re) - contract(einsum_form, table_im, value_im)
    out_im = contract(einsum_form, table_re, value_im) + contract(einsum_form, table_im, value_re)
    return (out_re, out_im)


def arrange_tiles(loaded, dest_tiles, tile_counts, devices):
    slot_count = dest_tiles.shape[0]
    chans_here = loaded.shape[2]
    tile_rows = loaded.shape[1] // slot_count
    per_pair = 4 * TILES_DEV // devices
    slot_ids = jnp.arange(slot_count, dtype=jnp.int32)
    valid_slot = slot_ids < tile_counts[0]
    owner_device = dest_tiles // TILES_DEV
    hit_table = (
        (owner_device[:, None] == jnp.arange(devices, dtype=jnp.int32)[None, :])
        & valid_slot[:, None]
    ).astype(jnp.int32)
    before = jnp.cumsum(hit_table, axis=0) - 1
    send_slot = owner_device * per_pair + jnp.sum(before * hit_table, axis=1)
    chosen = (
        send_slot[None, :] == jnp.arange(devices * per_pair, dtype=jnp.int32)[:, None]
    ) & valid_slot[None, :]
    slot_data = loaded.reshape(3, slot_count, tile_rows * chans_here)
    packed = jnp.einsum(
        "sj,ijx->isx", chosen.astype(jnp.bfloat16), slot_data, preferred_element_type=jnp.float32
    ).astype(jnp.bfloat16)
    local_ids = (dest_tiles % TILES_DEV).astype(jnp.float32)
    labels = jnp.where(
        jnp.any(chosen, axis=1), jnp.sum(jnp.where(chosen, local_ids[None, :], 0.0), axis=1), -1.0
    ).astype(jnp.bfloat16)
    received, tile_labels = (
        lax.all_to_all(
            packed.reshape(3, devices, per_pair, tile_rows * chans_here),
            "seq",
            split_axis=1,
            concat_axis=1,
            tiled=True,
        ),
        lax.all_to_all(
            labels.reshape(1, devices, per_pair), "seq", split_axis=1, concat_axis=1, tiled=True
        ),
    )
    pick_table = (
        tile_labels.reshape(-1)[None, :].astype(jnp.float32)
        == jnp.arange(TILES_DEV, dtype=jnp.float32)[:, None]
    ).astype(jnp.bfloat16)
    placed = jnp.einsum(
        "ts,isx->itx",
        pick_table,
        received.reshape(3, devices * per_pair, tile_rows * chans_here),
        preferred_element_type=jnp.float32,
    )
    return placed.astype(jnp.bfloat16).reshape(3, TILES_DEV * tile_rows, chans_here)


def sequence_conv(mixed_rows, kernels, devices):
    seq_rows, chans_here = mixed_rows.shape
    filter_count = kernels.shape[0]
    block_rows = seq_rows // devices
    period = 2 * seq_rows * devices
    position = lax.axis_index("seq")
    signal, kernel_part = (
        lax.all_to_all(
            mixed_rows.reshape(devices, block_rows, chans_here),
            "seq",
            split_axis=0,
            concat_axis=0,
            tiled=True,
        ),
        lax.all_to_all(
            kernels.T.reshape(devices, block_rows, filter_count),
            "seq",
            split_axis=0,
            concat_axis=0,
            tiled=True,
        ),
    )
    outer_angle = angles(
        jnp.arange(2 * devices, dtype=jnp.int32), jnp.arange(devices, dtype=jnp.int32), 2 * devices
    )
    outer_cos = jnp.cos(outer_angle)
    outer_sin = jnp.sin(outer_angle)
    local_index = position * block_rows + jnp.arange(block_rows, dtype=jnp.int32)
    twist_angle = angles(jnp.arange(2 * devices, dtype=jnp.int32), local_index, period)
    twist_cos = jnp.cos(twist_angle)[:, :, None]
    twist_sin = -jnp.sin(twist_angle)[:, :, None]

    def forward_outer(value_entries):
        real_in = value_entries.astype(jnp.float32)
        first_re = contract("kp,pmc->kmc", outer_cos, real_in)
        first_im = -contract("kp,pmc->kmc", outer_sin, real_in)
        rot_re = first_re * twist_cos - first_im * twist_sin
        rot_im = first_re * twist_sin + first_im * twist_cos
        stacked = jnp.stack([rot_re, rot_im])
        return stacked.reshape(2, devices, 2, block_rows, value_entries.shape[2])

    data_cols, kern_cols = (
        lax.all_to_all(forward_outer(signal), "seq", split_axis=1, concat_axis=3, tiled=True),
        lax.all_to_all(forward_outer(kernel_part), "seq", split_axis=1, concat_axis=3, tiled=True),
    )
    data_cols = data_cols.reshape(2, 2, seq_rows, chans_here)
    kern_cols = kern_cols.reshape(2, 2, seq_rows, filter_count)
    inner_angle = angles(
        jnp.arange(seq_rows, dtype=jnp.int32), jnp.arange(seq_rows, dtype=jnp.int32), seq_rows
    )
    inner_cos = jnp.cos(inner_angle)
    inner_sin = jnp.sin(inner_angle)
    spec_re, spec_im = complex_apply(
        "km,bmc->bkc", inner_cos, -inner_sin, data_cols[0], data_cols[1]
    )
    ker_re, ker_im = complex_apply("km,bmc->bkc", inner_cos, -inner_sin, kern_cols[0], kern_cols[1])
    ker_re = jnp.repeat(ker_re, chans_here // filter_count, axis=2)
    ker_im = jnp.repeat(ker_im, chans_here // filter_count, axis=2)
    prod_re = spec_re * ker_re - spec_im * ker_im
    prod_im = spec_re * ker_im + spec_im * ker_re
    back_re, back_im = complex_apply("mk,bkc->bmc", inner_cos, inner_sin, prod_re, prod_im)
    held_freq = 2 * position + jnp.arange(2, dtype=jnp.int32)
    untwist = angles(held_freq, jnp.arange(seq_rows, dtype=jnp.int32), period)
    untwist_cos = jnp.cos(untwist)[:, :, None]
    untwist_sin = jnp.sin(untwist)[:, :, None]
    rot_re = back_re * untwist_cos - back_im * untwist_sin
    rot_im = back_re * untwist_sin + back_im * untwist_cos
    stacked = jnp.stack([rot_re, rot_im]).reshape(2, 2, devices, block_rows, chans_here)
    gathered = lax.all_to_all(stacked, "seq", split_axis=2, concat_axis=1, tiled=True)
    final_angle = angles(
        jnp.arange(devices, dtype=jnp.int32), jnp.arange(2 * devices, dtype=jnp.int32), 2 * devices
    )
    result = (
        contract("pk,kmc->pmc", jnp.cos(final_angle), gathered[0, :, 0])
        - contract("pk,kmc->pmc", jnp.sin(final_angle), gathered[1, :, 0])
    ) / period
    returned = lax.all_to_all(result, "seq", split_axis=0, concat_axis=1, tiled=True)
    return returned.reshape(seq_rows, chans_here)


def local(
    loaded, dest_tiles, tile_counts, segments, short_filters, long_filters, skip_gain, norm_gain
):
    devices = lax.axis_size("seq")
    arranged = arrange_tiles(loaded, dest_tiles, tile_counts, devices)
    seq_rows = arranged.shape[1]
    chans_here = arranged.shape[2]
    reach_rows = short_filters.shape[1] - 1
    current = segments.astype(jnp.float32)
    rim_rows, rim_segments = from_behind(
        (
            arranged[:, seq_rows - reach_rows :, :].astype(jnp.float32),
            current[seq_rows - reach_rows :],
        ),
        "seq",
        1,
    )
    extended = jnp.concatenate([rim_rows.astype(jnp.bfloat16), arranged], axis=1)
    segment_ext = jnp.concatenate([rim_segments, current])
    filtered = jnp.zeros((3, seq_rows, chans_here), jnp.float32)
    for offset in range(reach_rows + 1):
        begin_row = reach_rows - offset
        window = extended[:, begin_row : begin_row + seq_rows, :].astype(jnp.float32)
        same_doc = segment_ext[begin_row : begin_row + seq_rows] == current
        filtered = (
            filtered
            + jnp.where(same_doc[None, :, None], window, 0.0)
            * short_filters[:, offset, :][:, None, :]
        )
    gate_rows = lax.optimization_barrier(filtered[0].astype(jnp.bfloat16))
    mixed_rows = lax.optimization_barrier((filtered[1] * filtered[2]).astype(jnp.bfloat16))
    convolved = sequence_conv(mixed_rows, long_filters, devices)
    gated_rows = gate_rows.astype(jnp.float32) * (
        convolved + skip_gain[None, :] * mixed_rows.astype(jnp.float32)
    )
    row_power = lax.psum(jnp.sum(gated_rows * gated_rows, axis=1), "chan") / CHANNELS
    return (gated_rows * lax.rsqrt(row_power + 1e-06)[:, None] * norm_gain[None, :]).astype(
        jnp.bfloat16
    )


def solution(mesh):
    return jax.shard_map(
        local,
        mesh=mesh,
        in_specs=(
            P(None, "seq", "chan"),
            P("seq"),
            P("seq"),
            P("seq"),
            P(None, None, "chan"),
            P("chan", "seq"),
            P("chan"),
            P("chan"),
        ),
        out_specs=P("seq", "chan"),
        check_vma=False,
    )
```

profile of v0, /device:TPU:11, one launch (start us, length us, event | category | flops | bytes accessed | tf_op | source)
XLA Modules:
  0.0 2007.9 jit_solution(13012017260324844309)
XLA Ops:
  9.1 15.5 reshape.233
  24.6 15.6 fusion
  40.2 29.0 %reshape.234 = bf16[3,16,4,65536]{3,2,1,0:T(4,128)(2,1)} reshape(bf16[3,64,65536]{2,1,0:T(8,128)(2,1)} %fusion) | data formatting | bytes 50331648 | tf_op jit(solution)/shard_map/reshape | solution.py:63
  69.2 17.2 copy.86
  97.1 535.2 %collective-permute-done = f32[6]{0:T(128)S(1)} collective-permute-done((f32[6]{0:T(128)S(1)}, f32[6]{0:T(128)S(1)}, u32[]{:S(2)}, u32[]{:S(2)}) %collective-permute-start) | collective-permute-done | bytes 56 | tf_op jit(solution)/shard_map/ppermute | solution.py:18
  639.4 17.2 copy.87
  656.7 27.9 %reshape.235 = bf16[3,64,65536]{2,1,0:T(8,128)(2,1)} reshape(bf16[3,16,4,65536]{3,2,1,0:T(4,128)(2,1)} %copy.87) | data formatting | bytes 50331648 | tf_op jit(solution)/shard_map/reshape | solution.py:80
  684.6 12.7 fusion.1
  697.3 8.1 reshape.236
  711.2 28.6 %multiply_add_fusion = f32[3,512,2048]{2,1,0:T(8,128)S(1)} fusion(bf16[3,512,2048]{2,1,0:T(8,128)(2,1)} %reshape.236, bf16[3,6,2048]{2,1,0:T(8,128)(2,1)S(1)} %collective-permute-done.1, f32[3,2048]{1,0:T(4,128)S(1)} %get-tuple-element.39, f32[3,2048]{1,0:T(4,128)S(1)} %get-tuple-element.40, f32[3,2048]{1,0:T(4,128)S(1)} %get-tuple-element.41, ...), kind=kLoop, calls=%fused_computation.16 | loop fusion | flops 141557760 | bytes 19123712 | tf_op jit(solution)/shard_map/add | solution.py:191
  746.2 7.0 all-to-all-start.2
  756.2 44.4 %all-to-all-done.2 = bf16[16,32,2048]{2,1,0:T(8,128)(2,1)S(1)} async-done(((bf16[16,32,2048]{2,1,0:T(8,128)(2,1)}), bf16[16,32,2048]{2,1,0:T(8,128)(2,1)S(1)}, u32[]{:S(2)}, u32[]{:S(2)}) %all-to-all-start.2) | async-done | bytes 2097184 | tf_op jit(solution)/shard_map/all_to_all | solution.py:93
  817.3 8.3 copy.129
  825.5 8.1 copy.130
  833.7 9.9 pad_maximum_fusion
  843.6 6.6 all-to-all-start.3
  875.2 337.0 %all-to-all-done.3 = f32[2,16,2,32,2048]{4,3,2,0,1:T(8,128)} async-done(((f32[2,16,2,32,2048]{4,3,2,0,1:T(8,128)}), f32[2,16,2,32,2048]{4,3,2,0,1:T(8,128)}, u32[]{:S(2)}, u32[]{:S(2)}) %all-to-all-start.3) | async-done | bytes 16777248 | tf_op jit(solution)/shard_map/all_to_all | solution.py:128
  1212.1 11.7 copy.168
  1230.3 37.6 %fusion.44 = f32[2,2048,512]{2,1,0:T(8,128)} fusion(f32[2,512,2048]{2,1,0:T(8,128)S(1)} %bitcast.163), kind=kOutput, calls=%fused_computation.82 | convolution fusion | flops 12888571904 | bytes 16777216 | tf_op jit(solution)/shard_map/km,bmc->bkc/dot_general | solution.py:22
  1267.9 37.8 %fusion.40 = f32[2,2048,512]{2,1,0:T(8,128)} fusion(f32[2,512,2048]{2,1,0:T(8,128)S(1)} %bitcast.161), kind=kOutput, calls=%fused_computation.78 | convolution fusion | flops 12888571904 | bytes 16777216 | tf_op jit(solution)/shard_map/km,bmc->bkc/dot_general | solution.py:22
  1305.6 38.3 %convolution_subtract_fusion.1 = f32[2,2048,512]{2,1,0:T(8,128)} fusion(f32[2,2048,512]{2,1,0:T(8,128)S(1)} %copy-done.3, f32[2,512,2048]{2,1,0:T(8,128)S(1)} %bitcast.162), kind=kOutput, calls=%fused_computation.47 | convolution fusion | flops 12890931200 | bytes 25165824 | tf_op jit(solution)/shard_map/km,bmc->bkc/dot_general | solution.py:22
  1343.9 40.1 %fusion.2 = (f32[2,512,2048]{1,2,0:T(8,128)}, f32[2,512,2048]{1,2,0:T(8,128)}) fusion(f32[2,2048,512]{2,1,0:T(8,128)} %convolution_subtract_fusion.1, f32[2,512,128]{1,2,0:T(8,128)S(1)} %fusion.23, f32[2,512,128]{1,2,0:T(8,128)S(1)} %fusion.24, f32[2,2048,512]{2,1,0:T(8,128)} %fusion.40, f32[2,512,2048]{2,1,0:T(8,128)} %bitcast.164), kind=kOutput, calls=%fused_computation.17 | convolution fusion | flops 12903514112 | bytes 42991616 | tf_op jit(solution)/shard_map/km,bmc->bkc/dot_general | solution.py:22
  1384.0 23.6 %fusion.36 = f32[2,2048,512]{1,2,0:T(8,128)S(1)} fusion(f32[2,512,2048]{1,2,0:T(8,128)} %get-tuple-element.5), kind=kOutput, calls=%fused_computation.74 | convolution fusion | flops 12888571904 | bytes 16777216 | tf_op jit(solution)/shard_map/mk,bkc->bmc/dot_general | solution.py:22
  1407.7 23.5 %fusion.34 = f32[2,2048,512]{1,2,0:T(8,128)} fusion(f32[2,512,2048]{1,2,0:T(8,128)S(1)} %copy-done), kind=kOutput, calls=%fused_computation.72 | convolution fusion | flops 12888571904 | bytes 16777216 | tf_op jit(solution)/shard_map/mk,bkc->bmc/dot_general | solution.py:22
  1431.1 21.5 %convolution_subtract_fusion = f32[2,2048,512]{1,2,0:T(8,128)} fusion(f32[2,2048,512]{1,2,0:T(8,128)S(1)} %fusion.36, f32[2,512,2048]{1,2,0:T(8,128)S(1)} %copy-done), kind=kOutput, calls=%fused_computation.45 | convolution fusion | flops 12890669056 | bytes 25165824 | tf_op jit(solution)/shard_map/mk,bkc->bmc/dot_general | solution.py:22
  1452.6 29.6 %multiply_subtract_fusion = (f32[2,2048,512]{1,2,0:T(8,128)}, f32[2,2048,512]{1,2,0:T(8,128)}) fusion(f32[2,2048,512]{1,2,0:T(8,128)} %convolution_subtract_fusion, f32[2,512]{1,0:T(2,128)S(1)} %get-tuple-element.34, f32[2,512]{1,0:T(2,128)S(1)} %get-tuple-element.33, f32[2,2048,512]{1,2,0:T(8,128)} %fusion.34, f32[2,512,2048]{1,2,0:T(8,128)} %get-tuple-element.5), kind=kOutput, calls=%fused_computation.24 | convolution fusion | flops 12903251968 | bytes 41951232 | tf_op jit(solution)/shard_map/mk,bkc->bmc/dot_general | solution.py:22
  1482.2 6.6 pad_maximum_fusion.1
  1494.8 366.8 %all_to_all.74 = f32[2,2,16,32,2048]{4,3,1,0,2:T(8,128)S(1)} all-to-all(f32[2,2,16,32,2048]{4,3,1,0,2:T(8,128)} %copy.131), channel_id=1, replica_groups=mesh['seq'=16,'chan'=2] {'seq'}, dimensions={2} | all-to-all | bytes 33554432 | tf_op jit(solution)/shard_map/all_to_all | solution.py:154
  1867.8 12.9 fusion.4
  1880.8 9.9 subtract_multiply_fusion
  1895.3 6.6 all-to-all-start.7
  1904.5 89.9 %all-to-all-done.7 = f32[16,32,2048]{2,1,0:T(8,128)} async-done(((f32[16,32,2048]{2,1,0:T(8,128)}), f32[16,32,2048]{2,1,0:T(8,128)}, u32[]{:S(2)}, u32[]{:S(2)}) %all-to-all-start.7) | async-done | bytes 4194336 | tf_op jit(solution)/shard_map/all_to_all | solution.py:162
  (85 shorter events, 121.9 us)
Async XLA Ops:
  2.5 84.0 %all-to-all-start.1 = ((bf16[1,16,4]{2,0,1:T(2,128)(2,1)}), bf16[1,16,4]{2,0,1:T(2,128)(2,1)S(1)}, u32[]{:S(2)}, u32[]{:S(2)}) async-start(bf16[1,16,4]{2,0,1:T(2,128)(2,1)} %convert_element_type.186), calls=%async_computation.1 | async-start | bytes 16384 | tf_op jit(solution)/shard_map/all_to_all | solution.py:69
  86.4 6.2 copy-start.9
  86.4 9.6 copy-start.6
  86.4 9.8 copy-start.7
  86.5 548.0 %all-to-all-start = ((bf16[3,16,4,65536]{3,2,0,1:T(4,128)(2,1)}), bf16[3,16,4,65536]{3,2,0,1:T(4,128)(2,1)}, u32[]{:S(2)}, u32[]{:S(2)}) async-start(bf16[3,16,4,65536]{3,2,0,1:T(4,128)(2,1)} %copy.86), calls=%async_computation | async-start | bytes 50331648 | tf_op jit(solution)/shard_map/all_to_all | solution.py:62
  92.7 539.6 %collective-permute-start = (f32[6]{0:T(128)S(1)}, f32[6]{0:T(128)S(1)}, u32[]{:S(2)}, u32[]{:S(2)}) collective-permute-start(f32[6]{0:T(128)S(1)} %slice.98), channel_id=1, source_target_pairs={{0,2},{2,4},{4,6},{6,8},{8,10},{10,12},{12,14},{14,16},{16,18},{18... | collective-permute-start | bytes 80 | tf_op jit(solution)/shard_map/ppermute | solution.py:18
  634.5 111.7 %all-to-all-start.4 = ((bf16[16,32,128]{2,1,0:T(8,128)(2,1)}), bf16[16,32,128]{2,1,0:T(8,128)(2,1)S(1)}, u32[]{:S(2)}, u32[]{:S(2)}) async-start(bf16[16,32,128]{2,1,0:T(8,128)(2,1)} %bitcast.22), calls=%async_computation.4 | async-start | bytes 262144 | tf_op jit(solution)/shard_map/all_to_all | solution.py:100
  706.3 5.0 collective-permute-start.1
  739.8 4.4 copy-start.2
  746.2 54.4 %all-to-all-start.2 = ((bf16[16,32,2048]{2,1,0:T(8,128)(2,1)}), bf16[16,32,2048]{2,1,0:T(8,128)(2,1)S(1)}, u32[]{:S(2)}, u32[]{:S(2)}) async-start(bf16[16,32,2048]{2,1,0:T(8,128)(2,1)} %bitcast.9), calls=%async_computation.2 | async-start | bytes 4194304 | tf_op jit(solution)/shard_map/all_to_all | solution.py:93
  800.6 42.9 %all-to-all-start.5 = ((f32[2,16,2,32,128]{4,3,2,0,1:T(8,128)}), f32[2,16,2,32,128]{4,3,2,0,1:T(8,128)}, u32[]{:S(2)}, u32[]{:S(2)}) async-start(f32[2,16,2,32,128]{4,3,2,0,1:T(8,128)} %pad_maximum_fusion.3), calls=%async_computation.5 | async-start | bytes 2097152 | tf_op jit(solution)/shard_map/all_to_all | solution.py:129
  825.5 8.1 copy-start.4
  843.6 368.5 %all-to-all-start.3 = ((f32[2,16,2,32,2048]{4,3,2,0,1:T(8,128)}), f32[2,16,2,32,2048]{4,3,2,0,1:T(8,128)}, u32[]{:S(2)}, u32[]{:S(2)}) async-start(f32[2,16,2,32,2048]{4,3,2,0,1:T(8,128)} %pad_maximum_fusion), calls=%async_computation.3 | async-start | bytes 33554432 | tf_op jit(solution)/shard_map/all_to_all | solution.py:128
  1230.2 37.6 %copy-start.1 = (f32[1,1,2,16,32,2048]{5,4,3,2,1,0:T(8,128)}, f32[1,1,2,16,32,2048]{5,4,3,2,1,0:T(8,128)S(1)}, u32[]{:S(2)}) copy-start(f32[1,1,2,16,32,2048]{5,4,3,2,1,0:T(8,128)S(1)} %get-tuple-element.13) | copy-start | bytes 25165828
  1267.8 37.8 %copy-start.3 = (f32[2,2048,512]{2,1,0:T(8,128)S(1)}, f32[2,2048,512]{2,1,0:T(8,128)}, u32[]{:S(2)}) copy-start(f32[2,2048,512]{2,1,0:T(8,128)} %fusion.44) | copy-start | bytes 25165828
  1384.0 23.6 %copy-start = (f32[2,512,2048]{1,2,0:T(8,128)S(1)}, f32[2,512,2048]{1,2,0:T(8,128)}, u32[]{:S(2)}) copy-start(f32[2,512,2048]{1,2,0:T(8,128)} %get-tuple-element.6) | copy-start | bytes 25165828
  1867.8 12.9 copy-start.5
  1895.3 99.1 %copy-start.8 = (f32[2048]{0:T(1024)S(1)}, f32[2048]{0:T(1024)}, u32[]{:S(2)}) copy-start(f32[2048]{0:T(1024)} %param.14) | copy-start | bytes 24580
  1895.3 99.1 %all-to-all-start.7 = ((f32[16,32,2048]{2,1,0:T(8,128)}), f32[16,32,2048]{2,1,0:T(8,128)}, u32[]{:S(2)}, u32[]{:S(2)}) async-start(f32[16,32,2048]{2,1,0:T(8,128)} %copy.116), calls=%async_computation.7 | async-start | bytes 8388608 | tf_op jit(solution)/shard_map/all_to_all | solution.py:162
  1901.9 100.1 %copy-start.10 = (f32[2048]{0:T(1024)S(1)}, f32[2048]{0:T(1024)}, u32[]{:S(2)}) copy-start(f32[2048]{0:T(1024)} %param.15) | copy-start | bytes 24580
where the time goes:
time: 2020 us; the launch traced here: 2010 us
  waiting for transfers between devices  1010 us (50%)
  blocking collectives  371 us (18%)
  matrix products  339 us (17%)
  local copies, waits for them, and re-layouts  178 us (9%)
  other arithmetic  58.9 us (3%)
  starting transfers between devices  50 us (2%)
    ppermute x2, waiting for transfers between devices, from_behind(): return lax.ppermute(block, axis, route)  537 us
    all_to_all x1, blocking collectives, sequence_conv(): lax.all_to_all(stacked, 'seq', split_axis=2, concat_axis=1, tiled=True)  367 us
    all_to_all x1, waiting for transfers between devices, sequence_conv(): lax.all_to_all(forward_outer(signal), 'seq', split_axis=1, concat_axis=3,...  337 us
    dot_general x18, matrix products, contract(): return jnp.einsum(einsum_form, left_side, right_side, precision=highest)  310 us
    all_to_all x1, waiting for transfers between devices, sequence_conv(): lax.all_to_all(result, 'seq', split_axis=0, concat_axis=1, tiled=True)  89.9 us
    reshape x2, local copies, waits for them, and re-layouts, arrange_tiles(): packed.reshape(3, devices, per_pair, tile_rows * chans_here)  46.2 us
    all_to_all x1, waiting for transfers between devices, sequence_conv(): lax.all_to_all(mixed_rows.reshape(devices, block_rows, chans_here), 'seq'...  44.4 us
  transfers between devices with their start and end apart: 9, of which 6 were waited for; matrix products, arithmetic and copies ran while one was open for 12% of the time, Pallas kernels for 0%

commit v1 on v0

v1 whole, which is shorter than its diff:
```python
import functools

import jax
import jax.numpy as jnp
from jax import lax
from jax.experimental import pallas as pl
from jax.experimental.pallas import tpu as pltpu
from jax.sharding import PartitionSpec as P

GROUP_SIZE = 16
TILE = 32
BLOCK = 256
LANES = 128
CHUNK = 1024


def place_and_filter(holder, recv, reach, taps, gate, mixed, cap, rows_r, tile):
    slot = holder[tile]
    back = holder[jnp.maximum(tile - 1, 0)]
    start = pl.multiple_of(lax.rem(slot, cap) * TILE, TILE)
    back_start = pl.multiple_of(lax.rem(back, cap) * TILE + TILE // 2, TILE // 2)
    source, back_source = slot // cap, back // cap
    row = pl.multiple_of(tile * TILE, TILE)
    limit = reach[pl.ds(row, TILE), :].astype(jnp.float32)
    results = []
    for r in rows_r:
        here = recv[source, r, pl.ds(start, TILE), :].astype(jnp.float32)
        before = recv[back_source, r, pl.ds(back_start, TILE // 2), :].astype(jnp.float32)
        ext = jnp.concatenate([before[TILE // 2 - 8 :], here], axis=0)
        total = here * taps[r, 0:1, :]
        for offset in range(1, 7):
            window = ext[8 - offset : 8 - offset + TILE]
            total = total + jnp.where(limit >= offset, window, 0.0) * taps[r, offset : offset + 1, :]
        results.append(total)
    return row, results


def long_conv(bands, toep, xt, yt, groups, blocks):
    seq = blocks * BLOCK
    toep[LANES:, 0:LANES] = jnp.zeros((LANES, LANES), toep.dtype)

    @pl.loop(0, groups)
    def _(g):
        @pl.loop(0, seq // CHUNK)
        def _(c):
            base = pl.multiple_of(c * CHUNK, CHUNK)
            part = bands[g, :, pl.ds(base, CHUNK + LANES)].astype(jnp.float32)
            for k in range(8):
                rolled = part if k == 0 else pltpu.roll(part, 16 * k, 1)
                rolled = rolled[:, LANES:].astype(toep.dtype)
                toep[16 * k : 16 * k + 16, pl.ds(base, CHUNK)] = rolled
                toep[LANES + 16 * k : LANES + 16 * k + 16, pl.ds(base + LANES, CHUNK)] = rolled

        yt[g] = jnp.zeros((blocks * GROUP_SIZE, BLOCK), jnp.float32)
        stages = 4
        for stage in range(stages):
            first = stage * blocks // stages
            rows = (blocks - first) * GROUP_SIZE

            @pl.loop(first, first + blocks // stages)
            def _(d):
                begin = pl.multiple_of(
                    (blocks + first - d) * GROUP_SIZE, GROUP_SIZE
                )
                lags = pl.multiple_of(d * BLOCK, BLOCK)
                yt[g, first * GROUP_SIZE :, :] += jnp.dot(
                    xt[g, pl.ds(begin, rows), :],
                    toep[:, pl.ds(lags, BLOCK)],
                    preferred_element_type=jnp.float32,
                )


def to_columns(mixed, xt, groups, block, blocks):
    row = pl.multiple_of(block * BLOCK, BLOCK)
    turned = mixed[pl.ds(row, BLOCK), :].astype(jnp.float32).T.astype(jnp.bfloat16)
    at = pl.multiple_of((blocks + block) * GROUP_SIZE, GROUP_SIZE)
    for g in range(groups):
        xt[g, pl.ds(at, GROUP_SIZE), :] = turned[g * GROUP_SIZE : (g + 1) * GROUP_SIZE]


def gate_block(gate, mixed, yt, skip, groups, block):
    row = pl.multiple_of(block * BLOCK, BLOCK)
    at = pl.multiple_of(block * GROUP_SIZE, GROUP_SIZE)
    parts = [yt[g, pl.ds(at, GROUP_SIZE), :] for g in range(groups)]
    if groups * GROUP_SIZE < LANES:
        parts.append(jnp.zeros((LANES - groups * GROUP_SIZE, BLOCK), jnp.float32))
    convolved = jnp.concatenate(parts, axis=0).T
    return gate[pl.ds(row, BLOCK), :].astype(jnp.float32) * (
        convolved + skip[...] * mixed[pl.ds(row, BLOCK), :].astype(jnp.float32)
    )


def operator_kernel(
    cap, groups, blocks, holder, recv, reach, taps, skip, bands, out, gate, mixed, xt, yt, toep
):
    tiles = BLOCK // TILE
    for g in range(groups):
        xt[g, 0 : blocks * GROUP_SIZE, :] = jnp.zeros((blocks * GROUP_SIZE, BLOCK), xt.dtype)

    @pl.loop(0, blocks)
    def _(block):
        @pl.loop(0, tiles)
        def _(i):
            row, (q, k, v) = place_and_filter(
                holder, recv, reach, taps, gate, mixed, cap, (0, 1, 2), block * tiles + i
            )
            gate[pl.ds(row, TILE), :] = q.astype(jnp.bfloat16)
            mixed[pl.ds(row, TILE), :] = (k * v).astype(jnp.bfloat16)

        to_columns(mixed, xt, groups, block, blocks)

    long_conv(bands, toep, xt, yt, groups, blocks)

    @pl.loop(0, blocks)
    def _(block):
        row = pl.multiple_of(block * BLOCK, BLOCK)
        out[pl.ds(row, BLOCK), :] = gate_block(gate, mixed, yt, skip, groups, block).astype(
            jnp.bfloat16
        )


def operator(holder, recv, reach, taps, skip, bands, cap, groups):
    seq = reach.shape[0]
    blocks = seq // BLOCK
    vmem = pl.BlockSpec(memory_space=pltpu.VMEM)
    return pl.pallas_call(
        functools.partial(operator_kernel, cap, groups, blocks),
        out_shape=jax.ShapeDtypeStruct((seq, LANES), jnp.bfloat16),
        in_specs=[pl.BlockSpec(memory_space=pltpu.SMEM)] + [vmem] * 5,
        out_specs=vmem,
        scratch_shapes=[
            pltpu.VMEM((seq, LANES), jnp.bfloat16),
            pltpu.VMEM((seq, LANES), jnp.bfloat16),
            pltpu.VMEM((groups, 2 * blocks * GROUP_SIZE, BLOCK), jnp.bfloat16),
            pltpu.VMEM((groups, blocks * GROUP_SIZE, BLOCK), jnp.float32),
            pltpu.VMEM((BLOCK, seq + LANES), jnp.bfloat16),
        ],
        compiler_params=pltpu.CompilerParams(vmem_limit_bytes=62 * 2**20),
    )(holder, recv, reach, taps, skip, bands)


def routing(dest_tiles, tile_counts, segments):
    cap = dest_tiles.shape[0]
    slots = lax.all_gather(dest_tiles, "seq", tiled=True)
    counts = lax.all_gather(tile_counts, "seq", tiled=True)
    docs = lax.all_gather(segments, "seq", tiled=True)
    seq = docs.shape[0]
    ids = jnp.arange(slots.shape[0], dtype=jnp.int32)
    used = ids % cap < jnp.repeat(counts, cap)
    hits = (slots[None, :] == jnp.arange(seq // TILE, dtype=jnp.int32)[:, None]) & used[None, :]
    holder = jnp.sum(jnp.where(hits, ids[None, :], 0), axis=1)
    reach = jnp.zeros((seq,), jnp.int32)
    for offset in range(1, 7):
        same = docs[offset:] == docs[: seq - offset]
        reach = reach + jnp.pad(same.astype(jnp.int32), (offset, 0))
    return holder, jnp.broadcast_to(reach.astype(jnp.bfloat16)[:, None], (seq, LANES))


def filter_bands(long_filters, devices, groups):
    count, lags = long_filters.shape
    if count < devices * groups:
        long_filters = jnp.repeat(long_filters, devices * groups // count, axis=0)
    mine = lax.all_to_all(long_filters, "seq", split_axis=0, concat_axis=1, tiled=True)
    seq = mine.shape[1]
    padded = jnp.pad(mine, ((0, 0), (LANES, 0)))
    shifted = [padded] + [jnp.pad(padded, ((0, 0), (s, 0)))[:, : seq + LANES] for s in range(1, 16)]
    return jnp.stack(shifted, axis=1)


def local(
    loaded, dest_tiles, tile_counts, segments, short_filters, long_filters, skip_gain, norm_gain
):
    devices = lax.axis_size("seq")
    chans_all = loaded.shape[2] * lax.axis_size("chan")
    chans_here = loaded.shape[2]
    width = chans_here // devices
    groups = max(1, width // GROUP_SIZE)
    rows = loaded.shape[1]
    cap = dest_tiles.shape[0]
    me = lax.axis_index("seq")
    pad = LANES - width
    holder, reach = routing(dest_tiles, tile_counts, segments)
    bands = filter_bands(long_filters, devices, groups)
    taps = lax.dynamic_slice_in_dim(short_filters, me * width, width, 2)
    taps = jnp.pad(taps, ((0, 0), (0, 1), (0, pad)))
    skip = jnp.pad(lax.dynamic_slice_in_dim(skip_gain, me * width, width, 0), (0, pad))[None, :]
    sliced = jnp.transpose(loaded.reshape(3, rows, devices, width), (2, 0, 1, 3))
    recv = lax.all_to_all(sliced, "seq", split_axis=0, concat_axis=0, tiled=True)
    recv = jnp.pad(recv, ((0, 0), (0, 0), (0, 0), (0, pad)))
    gated = operator(holder, recv, reach, taps, skip, bands, cap, groups)[:, :width]
    seq_rows = gated.shape[0] // devices
    back = lax.all_to_all(
        gated.reshape(devices, seq_rows, width), "seq", split_axis=0, concat_axis=0, tiled=True
    )
    gated_rows = jnp.transpose(back, (1, 0, 2)).reshape(seq_rows, chans_here).astype(jnp.float32)
    row_power = lax.psum(jnp.sum(gated_rows * gated_rows, axis=1), "chan") / chans_all
    return (gated_rows * lax.rsqrt(row_power + 1e-06)[:, None] * norm_gain[None, :]).astype(
        jnp.bfloat16
    )


def solution(mesh):
    return jax.shard_map(
        local,
        mesh=mesh,
        in_specs=(
            P(None, "seq", "chan"),
            P("seq"),
            P("seq"),
            P("seq"),
            P(None, None, "chan"),
            P("chan", "seq"),
            P("chan"),
            P("chan"),
        ),
        out_specs=P("seq", "chan"),
        check_vma=False,
    )
```

time: 2020 us -> 521 us (0.26)
  waiting for transfers between devices: 1010 us -> 0.01 us
  matrix products: 339 us -> 0 us
  local copies, waits for them, and re-layouts: 178 us -> 58.2 us
  Pallas kernels: 0 us -> 95.5 us
  other arithmetic: 58.9 us -> 3.74 us
  starting transfers between devices: 50 us -> 12.8 us
  blocking collectives: 371 us -> 345 us
    ppermute x2 -> x0, waiting for transfers between devices: 537 us -> none  [from_behind(): return lax.ppermute(block, axis, route)]
    all_to_all x7 -> x2, waiting for transfers between devices: 473 us -> 0.01 us  [the longest x1 0.01 us: filter_bands(): lax.all_to_all(long_filters, 'seq', split_axis=0, concat_axis=1, tiled=True)]
    dot_general x20 -> x0, matrix products: 339 us -> none  [the longest x18 310 us: contract(): return jnp.einsum(einsum_form, left_side, right_side, precision=highest)]
    all_to_all x1, blocking collectives: 367 us -> 55.8 us  [local(): lax.all_to_all(gated.reshape(devices, seq_rows, width), 'seq', split_axis...]
    unnamed x0 -> x1, blocking collectives: none -> 267 us
    pallas_call x0 -> x1, Pallas kernels: none -> 95.5 us  [operator(): pl.pallas_call(functools.partial(operator_kernel, cap, groups, blocks), o...]
    reshape x5 -> x2, local copies, waits for them, and re-layouts: 97.7 us -> 16.8 us  [the longest x1 16.7 us: local(): loaded.reshape(3, rows, devices, width)]
    all_to_all x7 -> x2, starting transfers between devices: 43.1 us -> 12.8 us  [the longest x1 6.69 us: filter_bands(): lax.all_to_all(long_filters, 'seq', split_axis=0, concat_axis=1, tiled=True)]
  transfers between devices with their start and end apart: 9 -> 2, of which waited for: 6 -> 0; matrix products, arithmetic and copies ran while one was open for 12% -> 11% of each run, Pallas kernels for 0% -> 0%
where the time goes in v1:
time: 521 us; the launch traced here: 517 us
  blocking collectives  345 us (66%)
  Pallas kernels  95.5 us (18%)
  local copies, waits for them, and re-layouts  58.2 us (11%)
  starting transfers between devices  12.8 us (2%)
    unnamed x1, blocking collectives  267 us
    pallas_call x1, Pallas kernels, operator(): pl.pallas_call(functools.partial(operator_kernel, cap, groups, blocks), o...  95.5 us
    all_to_all x1, blocking collectives, local(): lax.all_to_all(gated.reshape(devices, seq_rows, width), 'seq', split_axis...  55.8 us
    another operation x18, local copies, waits for them, and re-layouts, filter_bands(): return jnp.stack(shifted, axis=1)  18.9 us
    all_gather x1, blocking collectives, routing(): docs = lax.all_gather(segments, 'seq', tiled=True)  18.6 us
    unnamed x16, local copies, waits for them, and re-layouts  18.3 us
    reshape x1, local copies, waits for them, and re-layouts, local(): loaded.reshape(3, rows, devices, width)  16.7 us
  transfers between devices with their start and end apart: 2, of which 0 were waited for; matrix products, arithmetic and copies ran while one was open for 11% of the time, Pallas kernels for 0%

profile of v1, /device:TPU:11, one launch (start us, length us, event | category | flops | bytes accessed | tf_op | source)
XLA Modules:
  0.0 517.1 jit_solution(18387545422447610639)
XLA Ops:
  0.0 6.7 %all-to-all-start.1 = ((bf16[16,8,512]{2,1,0:T(8,128)(2,1)}), bf16[16,8,512]{2,1,0:T(8,128)(2,1)S(1)}, u32[]{:S(2)}, u32[]{:S(2)}) async-start(bf16[16,8,512]{2,1,0:T(8,128)(2,1)} %bitcast.65), calls=%async_computation.1 | async-start | bytes 262144 | tf_op jit(solution)/shard_map/all_to_all | solution.py:163
  6.7 16.7 %copy.333 = bf16[3,1024,2048]{1,2,0:T(8,128)(2,1)} copy(bf16[3,1024,2048]{2,1,0:T(8,128)(2,1)} %param.8) | data formatting | bytes 25165824 | tf_op args[0]
  23.4 16.7 %copy.334 = bf16[3,1024,16,128]{3,1,0,2:T(8,128)(2,1)} copy(bf16[3,1024,16,128]{1,3,2,0:T(8,128)(2,1)} %bitcast.56) | data formatting | bytes 25165824 | tf_op jit(solution)/shard_map/reshape | solution.py:187
  40.1 6.2 %all-to-all-start = ((bf16[16,3,1024,128]{3,2,1,0:T(8,128)(2,1)}), bf16[16,3,1024,128]{3,2,1,0:T(8,128)(2,1)}, u32[]{:S(2)}, u32[]{:S(2)}) async-start(bf16[16,3,1024,128]{3,2,1,0:T(8,128)(2,1)} %bitcast.55), calls=%async_computation | async-start | bytes 25165824 | tf_op jit(solution)/shard_map/all_to_all | solution.py:188
  46.9 0.6 dynamic-slice
  48.2 0.2 dynamic-update-slice
  48.4 0.8 dynamic-update-slice.1
  49.2 267.2 %all-reduce.25 = (s32[512]{0:T(512)S(1)}, s32[16]{0:T(128)S(1)}) all-reduce(s32[512]{0:T(512)S(1)} %dynamic-update-slice, s32[16]{0:T(128)S(1)} %dynamic-update-slice.1), channel_id=1, replica_groups=mesh['seq'=16,'chan'=2] {'seq'}, use_global_device_ids=true, to_apply=%add.23 | all-reduce | flops 528 | bytes 4224
  316.5 0.6 pad.122.taps
  317.1 18.6 %all-gather = s32[16,1,512]{2,1,0:T(1,128)S(1)} all-gather(s32[1,1,512]{2,1,0:T(1,128)S(1)} %bitcast.66), channel_id=1, replica_groups=mesh['seq'=16,'chan'=2] {'seq'}, dimensions={0}, use_global_device_ids=true | all-gather | bytes 34816 | tf_op jit(solution)/shard_map/all_gather | solution.py:146
  335.8 1.3 dynamic-slice_bitcast_fusion.skip
  337.7 0.8 select_reduce_fusion.holder
  338.5 0.2 copy.335
  338.7 0.6 fusion.18
  339.3 0.2 copy.336
  339.5 0.2 copy.337
  339.8 0.2 copy.338
  340.0 0.2 copy.339
  340.2 0.2 copy.340
  340.4 0.2 copy.341
  340.6 0.2 copy.342
  341.7 0.9 copy.347
  342.6 0.9 copy.348
  343.5 0.9 copy.349
  344.4 0.9 copy.350
  345.4 12.2 %stack.67.bands = bf16[8,16,8320]{2,1,0:T(8,128)(2,1)} concatenate(bf16[8,1,8320]{2,1,0:T(2,128)(2,1)S(1)} %copy.335, bf16[8,1,8320]{2,1,0:T(2,128)(2,1)S(1)} %copy.336, bf16[8,1,8320]{2,1,0:T(2,128)(2,1)S(1)} %copy.337, bf16[8,1,8320]{2,1,0:T(2,128)(2,1)S(1)} %copy.338, bf16[8,1,8320]{2,1,0:T(2,128)(2,1)S(1)} %copy.339, bf16[8,1,8320]{2,1,0:T(2,128)(2,1)S(1)} %copy.340, ...), dimensions={1} | concatenate | bytes 4259840 | tf_op jit(solution)/shard_map/stack | solution.py:167
  357.5 2.2 broadcast_in_dim.33.reach
  359.7 95.5 %shard_map.82 = bf16[8192,128]{1,0:T(8,128)(2,1)} custom-call(s32[256]{0:T(256)} %select_reduce_fusion.holder, bf16[16,3,1024,128]{3,2,1,0:T(8,128)(2,1)} %all-to-all-done.recv, bf16[8192,128]{1,0:T(8,128)(2,1)} %broadcast_in_dim.33.reach, f32[3,8,128]{2,1,0:T(8,128)} %pad.122.taps, f32[1,128]{1,0:T(1,128)} %dynamic-slice_bitcast_fusion.skip, ...), custom_call_target="tpu_custom_call" | custom-call | tf_op jit(solution)/shard_map/pallas_call | solution.py:126
  455.2 55.8 %all_to_all.29 = bf16[16,512,128]{2,1,0:T(8,128)(2,1)S(1)} all-to-all(bf16[16,512,128]{2,1,0:T(8,128)(2,1)} %bitcast.57), channel_id=1, replica_groups=mesh['seq'=16,'chan'=2] {'seq'}, dimensions={0} | all-to-all | bytes 4194304 | tf_op jit(solution)/shard_map/all_to_all | solution.py:192
  511.0 0.5 fusion
  511.4 3.8 psum.7
  515.2 1.9 fusion.2
  (31 shorter events, 1.6 us)
Async XLA Ops:
  0.0 316.5 %copy-start = (f32[3,7,2048]{2,1,0:T(8,128)S(1)}, f32[3,7,2048]{2,1,0:T(8,128)}, u32[]{:S(2)}) copy-start(f32[3,7,2048]{2,1,0:T(8,128)} %param.12) | copy-start | bytes 516100
  0.0 40.1 %all-to-all-start.1 = ((bf16[16,8,512]{2,1,0:T(8,128)(2,1)}), bf16[16,8,512]{2,1,0:T(8,128)(2,1)S(1)}, u32[]{:S(2)}, u32[]{:S(2)}) async-start(bf16[16,8,512]{2,1,0:T(8,128)(2,1)} %bitcast.65), calls=%async_computation.1 | async-start | bytes 262144 | tf_op jit(solution)/shard_map/all_to_all | solution.py:163
  40.1 6.8 %copy-start.4 = (u32[32]{0:T(128)S(1)}, u32[32]{0:T(128)}, u32[]{:S(2)}) copy-start(u32[32]{0:T(128)} %constant.88) | copy-start | bytes 388
  40.1 8.1 %copy-start.3 = (s32[32]{0:T(128)S(1)}, s32[32]{0:T(128)}, u32[]{:S(2)}) copy-start(s32[32]{0:T(128)} %param.9) | copy-start | bytes 388
  40.1 277.1 %copy-start.2 = (s32[512]{0:T(512)S(1)}, s32[512]{0:T(512)}, u32[]{:S(2)}) copy-start(s32[512]{0:T(512)} %param.11) | copy-start | bytes 6148
  40.1 317.4 %all-to-all-start = ((bf16[16,3,1024,128]{3,2,1,0:T(8,128)(2,1)}), bf16[16,3,1024,128]{3,2,1,0:T(8,128)(2,1)}, u32[]{:S(2)}, u32[]{:S(2)}) async-start(bf16[16,3,1024,128]{3,2,1,0:T(8,128)(2,1)} %bitcast.55), calls=%async_computation | async-start | bytes 25165824 | tf_op jit(solution)/shard_map/all_to_all | solution.py:188
  455.2 60.1 %copy-start.1 = (f32[2048]{0:T(1024)S(1)}, f32[2048]{0:T(1024)}, u32[]{:S(2)}) copy-start(f32[2048]{0:T(1024)} %param.15) | copy-start | bytes 24580

commit v2 on v1

--- a/solution.py
+++ b/solution.py
@@ -14,18 +14,16 @@
 CHUNK = 1024
 
 
-def place_and_filter(holder, recv, reach, taps, gate, mixed, cap, rows_r, tile):
-    slot = holder[tile]
-    back = holder[jnp.maximum(tile - 1, 0)]
-    start = pl.multiple_of(lax.rem(slot, cap) * TILE, TILE)
-    back_start = pl.multiple_of(lax.rem(back, cap) * TILE + TILE // 2, TILE // 2)
-    source, back_source = slot // cap, back // cap
+def place_and_filter(holder, recv, reach, taps, arrays, first, tile):
+    back = jnp.maximum(tile - 1, 0)
+    source, slot = holder[0, tile], holder[1, tile]
+    back_source, back_slot = holder[0, back], holder[1, back]
     row = pl.multiple_of(tile * TILE, TILE)
     limit = reach[pl.ds(row, TILE), :].astype(jnp.float32)
     results = []
-    for r in rows_r:
-        here = recv[source, r, pl.ds(start, TILE), :].astype(jnp.float32)
-        before = recv[back_source, r, pl.ds(back_start, TILE // 2), :].astype(jnp.float32)
+    for r in arrays:
+        here = recv[source, r - first, slot, :, :].astype(jnp.float32)
+        before = recv[back_source, r - first, back_slot, TILE // 2 :, :].astype(jnp.float32)
         ext = jnp.concatenate([before[TILE // 2 - 8 :], here], axis=0)
         total = here * taps[r, 0:1, :]
         for offset in range(1, 7):
@@ -91,7 +89,7 @@
 
 
 def operator_kernel(
-    cap, groups, blocks, holder, recv, reach, taps, skip, bands, out, gate, mixed, xt, yt, toep
+    groups, blocks, holder, recv, reach, taps, skip, bands, out, gate, mixed, xt, yt, toep
 ):
     tiles = BLOCK // TILE
     for g in range(groups):
@@ -102,7 +100,7 @@
         @pl.loop(0, tiles)
         def _(i):
             row, (q, k, v) = place_and_filter(
-                holder, recv, reach, taps, gate, mixed, cap, (0, 1, 2), block * tiles + i
+                holder, recv, reach, taps, (0, 1, 2), 0, block * tiles + i
             )
             gate[pl.ds(row, TILE), :] = q.astype(jnp.bfloat16)
             mixed[pl.ds(row, TILE), :] = (k * v).astype(jnp.bfloat16)
@@ -119,12 +117,12 @@
         )
 
 
-def operator(holder, recv, reach, taps, skip, bands, cap, groups):
+def operator(holder, recv, reach, taps, skip, bands, groups):
     seq = reach.shape[0]
     blocks = seq // BLOCK
     vmem = pl.BlockSpec(memory_space=pltpu.VMEM)
     return pl.pallas_call(
-        functools.partial(operator_kernel, cap, groups, blocks),
+        functools.partial(operator_kernel, groups, blocks),
         out_shape=jax.ShapeDtypeStruct((seq, LANES), jnp.bfloat16),
         in_specs=[pl.BlockSpec(memory_space=pltpu.SMEM)] + [vmem] * 5,
         out_specs=vmem,
@@ -139,20 +137,187 @@
     )(holder, recv, reach, taps, skip, bands)
 
 
+def exchange_kernel(
+    blocks, axis_peers, holder, loaded, reach, taps, skip, bands, out,
+    recv_q, recv_kv, mixed, xt, yt, toep, gated,
+    kv_send, kv_recv, q_send, q_recv, back_send, back_recv, own_sem,
+):
+    devices = axis_peers
+    me = lax.axis_index("seq")
+    groups = LANES // GROUP_SIZE
+    tiles = BLOCK // TILE
+    seq_rows = blocks * BLOCK // devices
+    per_device = seq_rows // BLOCK
+
+    def peer_at(k):
+        return lax.rem(me + k, devices)
+
+    def lanes_of(index):
+        return pl.ds(pl.multiple_of(index * LANES, LANES), LANES)
+
+    def kv_copy(k):
+        return pltpu.make_async_remote_copy(
+            src_ref=loaded.at[1:3, :, :, lanes_of(peer_at(k))],
+            dst_ref=recv_kv.at[me],
+            send_sem=kv_send.at[k],
+            recv_sem=kv_recv.at[k],
+            device_id={"seq": peer_at(k)},
+            device_id_type=pl.DeviceIdType.MESH,
+        )
+
+    def q_copy(k):
+        return pltpu.make_async_remote_copy(
+            src_ref=loaded.at[0:1, :, :, lanes_of(peer_at(k))],
+            dst_ref=recv_q.at[me],
+            send_sem=q_send.at[k],
+            recv_sem=q_recv.at[k],
+            device_id={"seq": peer_at(k)},
+            device_id_type=pl.DeviceIdType.MESH,
+        )
+
+    def rows_of(index):
+        return pl.ds(pl.multiple_of(index * seq_rows, seq_rows), seq_rows)
+
+    def back_copy(k):
+        return pltpu.make_async_remote_copy(
+            src_ref=gated.at[rows_of(peer_at(k))],
+            dst_ref=out.at[:, lanes_of(me)],
+            send_sem=back_send.at[k],
+            recv_sem=back_recv.at[k],
+            device_id={"seq": peer_at(k)},
+            device_id_type=pl.DeviceIdType.MESH,
+        )
+
+    barrier = pltpu.get_barrier_semaphore()
+
+    @pl.loop(1, devices)
+    def _(k):
+        pl.semaphore_signal(
+            barrier, inc=1, device_id={"seq": peer_at(k)}, device_id_type=pl.DeviceIdType.MESH
+        )
+
+    pl.semaphore_wait(barrier, devices - 1)
+
+    own_kv = pltpu.make_async_copy(
+        loaded.at[1:3, :, :, lanes_of(me)], recv_kv.at[me], own_sem.at[0]
+    )
+    own_q = pltpu.make_async_copy(loaded.at[0:1, :, :, lanes_of(me)], recv_q.at[me], own_sem.at[1])
+    own_back = pltpu.make_async_copy(gated.at[rows_of(me)], out.at[:, lanes_of(me)], own_sem.at[2])
+
+    @pl.loop(1, devices)
+    def _(k):
+        kv_copy(k).start()
+
+    own_kv.start()
+    own_q.start()
+    for g in range(groups):
+        xt[g, 0 : blocks * GROUP_SIZE, :] = jnp.zeros((blocks * GROUP_SIZE, BLOCK), xt.dtype)
+
+    @pl.loop(1, devices)
+    def _(k):
+        kv_copy(k).wait_send()
+        q_copy(k).start()
+
+    own_kv.wait()
+
+    @pl.loop(1, devices)
+    def _(k):
+        kv_copy(k).wait_recv()
+
+    @pl.loop(0, blocks)
+    def _(block):
+        @pl.loop(0, tiles)
+        def _(i):
+            row, (k, v) = place_and_filter(
+                holder, recv_kv, reach, taps, (1, 2), 1, block * tiles + i
+            )
+            mixed[pl.ds(row, TILE), :] = (k * v).astype(jnp.bfloat16)
+
+        to_columns(mixed, xt, groups, block, blocks)
+
+    long_conv(bands, toep, xt, yt, groups, blocks)
+
+    own_q.wait()
+
+    @pl.loop(1, devices)
+    def _(k):
+        q_copy(k).wait()
+
+    def gate_rows_of(owner):
+        for part in range(per_device):
+            block = owner * per_device + part
+
+            @pl.loop(0, tiles)
+            def _(i):
+                row, (q,) = place_and_filter(
+                    holder, recv_q, reach, taps, (0,), 0, block * tiles + i
+                )
+                gated[pl.ds(row, TILE), :] = q.astype(jnp.bfloat16)
+
+            row = pl.multiple_of(block * BLOCK, BLOCK)
+            gated[pl.ds(row, BLOCK), :] = gate_block(
+                gated, mixed, yt, skip, groups, block
+            ).astype(jnp.bfloat16)
+
+    @pl.loop(1, devices)
+    def _(k):
+        gate_rows_of(peer_at(k))
+        back_copy(k).start()
+
+    gate_rows_of(me)
+    own_back.start()
+    own_back.wait()
+
+    @pl.loop(1, devices)
+    def _(k):
+        back_copy(k).wait()
+
+
+def exchange_operator(holder, loaded, reach, taps, skip, bands, devices):
+    seq = reach.shape[0]
+    blocks = seq // BLOCK
+    groups = LANES // GROUP_SIZE
+    cap = loaded.shape[1]
+    vmem = pl.BlockSpec(memory_space=pltpu.VMEM)
+    anywhere = pl.BlockSpec(memory_space=pl.ANY)
+    dma = pltpu.SemaphoreType.DMA
+    return pl.pallas_call(
+        functools.partial(exchange_kernel, blocks, devices),
+        out_shape=jax.ShapeDtypeStruct((seq // devices, loaded.shape[3]), jnp.bfloat16),
+        in_specs=[pl.BlockSpec(memory_space=pltpu.SMEM), anywhere] + [vmem] * 4,
+        out_specs=anywhere,
+        scratch_shapes=[
+            pltpu.VMEM((devices, 1, cap, TILE, LANES), jnp.bfloat16),
+            pltpu.VMEM((devices, 2, cap, TILE, LANES), jnp.bfloat16),
+            pltpu.VMEM((seq, LANES), jnp.bfloat16),
+            pltpu.VMEM((groups, 2 * blocks * GROUP_SIZE, BLOCK), jnp.bfloat16),
+            pltpu.VMEM((groups, blocks * GROUP_SIZE, BLOCK), jnp.float32),
+            pltpu.VMEM((BLOCK, seq + LANES), jnp.bfloat16),
+            pltpu.VMEM((seq, LANES), jnp.bfloat16),
+        ]
+        + [dma((devices,))] * 6
+        + [dma((3,))],
+        compiler_params=pltpu.CompilerParams(
+            vmem_limit_bytes=60 * 2**20, collective_id=0, has_side_effects=True
+        ),
+    )(holder, loaded, reach, taps, skip, bands)
+
+
 def routing(dest_tiles, tile_counts, segments):
     cap = dest_tiles.shape[0]
-    slots = lax.all_gather(dest_tiles, "seq", tiled=True)
-    counts = lax.all_gather(tile_counts, "seq", tiled=True)
-    docs = lax.all_gather(segments, "seq", tiled=True)
+    marked = jnp.where(jnp.arange(cap, dtype=jnp.int32) < tile_counts[0], dest_tiles, -1)
+    gathered = lax.all_gather(jnp.concatenate([segments, marked]), "seq")
+    docs = gathered[:, : segments.shape[0]].reshape(-1)
+    slots = gathered[:, segments.shape[0] :].reshape(-1)
     seq = docs.shape[0]
     ids = jnp.arange(slots.shape[0], dtype=jnp.int32)
-    used = ids % cap < jnp.repeat(counts, cap)
-    hits = (slots[None, :] == jnp.arange(seq // TILE, dtype=jnp.int32)[:, None]) & used[None, :]
+    hits = slots[None, :] == jnp.arange(seq // TILE, dtype=jnp.int32)[:, None]
     holder = jnp.sum(jnp.where(hits, ids[None, :], 0), axis=1)
     reach = jnp.zeros((seq,), jnp.int32)
     for offset in range(1, 7):
         same = docs[offset:] == docs[: seq - offset]
         reach = reach + jnp.pad(same.astype(jnp.int32), (offset, 0))
+    holder = jnp.stack([holder // cap, holder % cap])
     return holder, jnp.broadcast_to(reach.astype(jnp.bfloat16)[:, None], (seq, LANES))
 
 
@@ -184,15 +349,21 @@
     taps = lax.dynamic_slice_in_dim(short_filters, me * width, width, 2)
     taps = jnp.pad(taps, ((0, 0), (0, 1), (0, pad)))
     skip = jnp.pad(lax.dynamic_slice_in_dim(skip_gain, me * width, width, 0), (0, pad))[None, :]
-    sliced = jnp.transpose(loaded.reshape(3, rows, devices, width), (2, 0, 1, 3))
-    recv = lax.all_to_all(sliced, "seq", split_axis=0, concat_axis=0, tiled=True)
-    recv = jnp.pad(recv, ((0, 0), (0, 0), (0, 0), (0, pad)))
-    gated = operator(holder, recv, reach, taps, skip, bands, cap, groups)[:, :width]
-    seq_rows = gated.shape[0] // devices
-    back = lax.all_to_all(
-        gated.reshape(devices, seq_rows, width), "seq", split_axis=0, concat_axis=0, tiled=True
-    )
-    gated_rows = jnp.transpose(back, (1, 0, 2)).reshape(seq_rows, chans_here).astype(jnp.float32)
+    if width == LANES:
+        tiled = loaded.reshape(3, cap, TILE, chans_here)
+        arrived = exchange_operator(holder, tiled, reach, taps, skip, bands, devices)
+    else:
+        sliced = jnp.transpose(loaded.reshape(3, rows, devices, width), (2, 0, 1, 3))
+        recv = lax.all_to_all(sliced, "seq", split_axis=0, concat_axis=0, tiled=True)
+        recv = jnp.pad(recv, ((0, 0), (0, 0), (0, 0), (0, pad)))
+        recv = recv.reshape(devices, 3, cap, TILE, LANES)
+        gated = operator(holder, recv, reach, taps, skip, bands, groups)[:, :width]
+        seq_rows = gated.shape[0] // devices
+        back = lax.all_to_all(
+            gated.reshape(devices, seq_rows, width), "seq", split_axis=0, concat_axis=0, tiled=True
+        )
+        arrived = jnp.transpose(back, (1, 0, 2)).reshape(seq_rows, chans_here)
+    gated_rows = arrived.astype(jnp.float32)
     row_power = lax.psum(jnp.sum(gated_rows * gated_rows, axis=1), "chan") / chans_all
     return (gated_rows * lax.rsqrt(row_power + 1e-06)[:, None] * norm_gain[None, :]).astype(
         jnp.bfloat16

time: 521 us -> 457 us (0.88)
  blocking collectives: 345 us -> 48.2 us
  Pallas kernels: 95.5 us -> 365 us
  local copies, waits for them, and re-layouts: 58.2 us -> 26 us
  starting transfers between devices: 12.8 us -> 6.69 us
    pallas_call x1, Pallas kernels: 95.5 us -> 365 us  [exchange_operator(): pl.pallas_call(functools.partial(exchange_kernel, blocks, devices), out_s...]
    unnamed x1, blocking collectives: 267 us -> 44.4 us
    all_to_all x1 -> x0, blocking collectives: 55.8 us -> none  [local(): lax.all_to_all(gated.reshape(devices, seq_rows, width), 'seq', split_axis...]
    all_gather x1 -> x0, blocking collectives: 18.6 us -> none  [routing(): docs = lax.all_gather(segments, 'seq', tiled=True)]
    unnamed x16 -> x8, local copies, waits for them, and re-layouts: 18.3 us -> 1.27 us
    reshape x2 -> x0, local copies, waits for them, and re-layouts: 16.8 us -> none  [the longest x1 16.7 us: local(): loaded.reshape(3, rows, devices, width)]
    all_to_all x1 -> x0, starting transfers between devices: 6.16 us -> none  [local(): lax.all_to_all(sliced, 'seq', split_axis=0, concat_axis=0, tiled=True)]
  transfers between devices with their start and end apart: 2 -> 1, of which waited for: 0 -> 0; matrix products, arithmetic and copies ran while one was open for 11% -> 1% of each run, Pallas kernels for 0% -> 0%
where the time goes in v2:
time: 457 us; the launch traced here: 456 us
  Pallas kernels  365 us (80%)
  blocking collectives  48.2 us (11%)
  local copies, waits for them, and re-layouts  26 us (6%)
  other arithmetic  8.33 us (2%)
  starting transfers between devices  6.69 us (1%)
    pallas_call x1, Pallas kernels, exchange_operator(): pl.pallas_call(functools.partial(exchange_kernel, blocks, devices), out_s...  365 us
    unnamed x1, blocking collectives  44.4 us
    another operation x18, local copies, waits for them, and re-layouts, filter_bands(): return jnp.stack(shifted, axis=1)  20.4 us
  transfers between devices with their start and end apart: 1, of which 0 were waited for; matrix products, arithmetic and copies ran while one was open for 1% of the time, Pallas kernels for 0%

profile of v2, /device:TPU:11, one launch (start us, length us, event | category | flops | bytes accessed | tf_op | source)
XLA Modules:
  0.0 455.6 jit_solution(14536859703175594030)
XLA Ops:
  0.0 6.7 %all-to-all-start = ((bf16[16,8,512]{2,1,0:T(8,128)(2,1)}), bf16[16,8,512]{2,1,0:T(8,128)(2,1)S(1)}, u32[]{:S(2)}, u32[]{:S(2)}) async-start(bf16[16,8,512]{2,1,0:T(8,128)(2,1)} %bitcast.54), calls=%async_computation | async-start | bytes 262144 | tf_op jit(solution)/shard_map/all_to_all | solution.py:328
  7.3 1.2 dynamic-slice
  9.2 0.7 compare_select_fusion.3
  9.9 0.8 add_dynamic-update-slice_fusion
  10.7 44.4 %all-reduce.23 = s32[8704]{0:T(1024)S(1)} all-reduce(s32[8704]{0:T(1024)S(1)} %add_dynamic-update-slice_fusion), channel_id=2, replica_groups=mesh['seq'=16,'chan'=2] {'seq'}, use_global_device_ids=true, to_apply=%add.23 | all-reduce | flops 8704 | bytes 69632
  55.8 0.1 select_reduce_fusion
  56.0 1.3 dynamic-slice_bitcast_fusion.skip
  57.3 0.6 pad.122.taps
  57.9 0.6 pad_add_fusion.holder
  58.7 0.6 fusion.17
  59.3 0.2 copy.266
  59.5 0.2 copy.267
  59.7 0.2 copy.268
  59.9 0.2 copy.269
  60.1 0.2 copy.270
  60.3 0.2 copy.271
  60.6 0.2 copy.272
  60.8 0.2 copy.273
  61.0 0.2 copy.274
  61.2 0.2 copy.275
  61.4 0.2 copy.276
  61.6 0.2 copy.277
  61.8 0.9 copy.278
  62.8 0.9 copy.279
  63.7 0.9 copy.280
  64.6 0.9 copy.265
  65.5 13.7 %stack.73.bands = bf16[8,16,8320]{2,1,0:T(8,128)(2,1)} concatenate(bf16[8,1,8320]{2,1,0:T(2,128)(2,1)} %copy.265, bf16[8,1,8320]{2,1,0:T(2,128)(2,1)S(1)} %copy.266, bf16[8,1,8320]{2,1,0:T(2,128)(2,1)S(1)} %copy.267, bf16[8,1,8320]{2,1,0:T(2,128)(2,1)S(1)} %copy.268, bf16[8,1,8320]{2,1,0:T(2,128)(2,1)S(1)} %copy.269, bf16[8,1,8320]{2,1,0:T(2,128)(2,1)S(1)} %copy.270, ...), dimensions={1} | concatenate | bytes 4259840 | tf_op jit(solution)/shard_map/stack | solution.py:332
  79.2 2.2 broadcast_in_dim.32.reach
  81.4 364.9 %shard_map.82 = bf16[512,2048]{1,0:T(8,128)(2,1)} custom-call(s32[2,256]{1,0:T(2,128)} %pad_add_fusion.holder, bf16[3,32,32,2048]{3,2,1,0:T(8,128)(2,1)} %bitcast.46, bf16[8192,128]{1,0:T(8,128)(2,1)} %broadcast_in_dim.32.reach, f32[3,8,128]{2,1,0:T(8,128)} %pad.122.taps, f32[1,128]{1,0:T(1,128)} %dynamic-slice_bitcast_fusion.skip, ...), custom_call_target="tpu_custom_call" | custom-call | tf_op jit(solution)/shard_map/pallas_call | solution.py:284
  446.3 2.1 fusion
  448.4 3.8 psum.7
  452.2 3.5 fusion.2
  (23 shorter events, 0.9 us)
Async XLA Ops:
  0.0 56.0 %copy-start = (f32[3,7,2048]{2,1,0:T(8,128)S(1)}, f32[3,7,2048]{2,1,0:T(8,128)}, u32[]{:S(2)}) copy-start(f32[3,7,2048]{2,1,0:T(8,128)} %param.12) | copy-start | bytes 516100
  0.0 58.6 %all-to-all-start = ((bf16[16,8,512]{2,1,0:T(8,128)(2,1)}), bf16[16,8,512]{2,1,0:T(8,128)(2,1)S(1)}, u32[]{:S(2)}, u32[]{:S(2)}) async-start(bf16[16,8,512]{2,1,0:T(8,128)(2,1)} %bitcast.54), calls=%async_computation | async-start | bytes 262144 | tf_op jit(solution)/shard_map/all_to_all | solution.py:328
  81.4 370.8 %copy-start.1 = (f32[2048]{0:T(1024)S(1)}, f32[2048]{0:T(1024)}, u32[]{:S(2)}) copy-start(f32[2048]{0:T(1024)} %param.15) | copy-start | bytes 24580

commit v3 on v2

--- a/solution.py
+++ b/solution.py
@@ -33,22 +33,23 @@
     return row, results
 
 
-def long_conv(bands, toep, xt, yt, groups, blocks):
-    seq = blocks * BLOCK
-    toep[LANES:, 0:LANES] = jnp.zeros((LANES, LANES), toep.dtype)
-
+def toeplitz(lags, toep, groups, blocks):
     @pl.loop(0, groups)
     def _(g):
-        @pl.loop(0, seq // CHUNK)
+        toep[g, :, 0:LANES] = jnp.zeros((LANES, LANES), toep.dtype)
+
+        @pl.loop(0, blocks * BLOCK // CHUNK)
         def _(c):
             base = pl.multiple_of(c * CHUNK, CHUNK)
-            part = bands[g, :, pl.ds(base, CHUNK + LANES)].astype(jnp.float32)
-            for k in range(8):
-                rolled = part if k == 0 else pltpu.roll(part, 16 * k, 1)
-                rolled = rolled[:, LANES:].astype(toep.dtype)
-                toep[16 * k : 16 * k + 16, pl.ds(base, CHUNK)] = rolled
-                toep[LANES + 16 * k : LANES + 16 * k + 16, pl.ds(base + LANES, CHUNK)] = rolled
-
+            part = lags[pl.ds(g, 1), pl.ds(base, CHUNK + LANES)]
+            part = jnp.broadcast_to(part, (LANES, CHUNK + LANES))
+            rolled = pltpu.roll(part, 0, 1, stride=1, stride_axis=0)
+            toep[g, :, pl.ds(base + LANES, CHUNK)] = rolled[:, LANES:].astype(toep.dtype)
+
+
+def long_conv(toep, xt, yt, groups, blocks):
+    @pl.loop(0, groups)
+    def _(g):
         yt[g] = jnp.zeros((blocks * GROUP_SIZE, BLOCK), jnp.float32)
         stages = 4
         for stage in range(stages):
@@ -57,14 +58,13 @@
 
             @pl.loop(first, first + blocks // stages)
             def _(d):
-                begin = pl.multiple_of(
-                    (blocks + first - d) * GROUP_SIZE, GROUP_SIZE
+                begin = pl.multiple_of((blocks + first - d) * GROUP_SIZE, GROUP_SIZE)
+                lag = pl.multiple_of(d * BLOCK, BLOCK)
+                table = jnp.concatenate(
+                    [toep[g, :, pl.ds(lag + LANES, BLOCK)], toep[g, :, pl.ds(lag, BLOCK)]], axis=0
                 )
-                lags = pl.multiple_of(d * BLOCK, BLOCK)
                 yt[g, first * GROUP_SIZE :, :] += jnp.dot(
-                    xt[g, pl.ds(begin, rows), :],
-                    toep[:, pl.ds(lags, BLOCK)],
-                    preferred_element_type=jnp.float32,
+                    xt[g, pl.ds(begin, rows), :], table, preferred_element_type=jnp.float32
                 )
 
 
@@ -89,7 +89,7 @@
 
 
 def operator_kernel(
-    groups, blocks, holder, recv, reach, taps, skip, bands, out, gate, mixed, xt, yt, toep
+    groups, blocks, holder, recv, reach, taps, skip, lags, out, gate, mixed, xt, yt, toep
 ):
     tiles = BLOCK // TILE
     for g in range(groups):
@@ -97,7 +97,7 @@
 
     @pl.loop(0, blocks)
     def _(block):
-        @pl.loop(0, tiles)
+        @pl.loop(0, tiles, unroll=4)
         def _(i):
             row, (q, k, v) = place_and_filter(
                 holder, recv, reach, taps, (0, 1, 2), 0, block * tiles + i
@@ -107,7 +107,8 @@
 
         to_columns(mixed, xt, groups, block, blocks)
 
-    long_conv(bands, toep, xt, yt, groups, blocks)
+    toeplitz(lags, toep, groups, blocks)
+    long_conv(toep, xt, yt, groups, blocks)
 
     @pl.loop(0, blocks)
     def _(block):
@@ -117,7 +118,7 @@
         )
 
 
-def operator(holder, recv, reach, taps, skip, bands, groups):
+def operator(holder, recv, reach, taps, skip, lags, groups):
     seq = reach.shape[0]
     blocks = seq // BLOCK
     vmem = pl.BlockSpec(memory_space=pltpu.VMEM)
@@ -131,16 +132,16 @@
             pltpu.VMEM((seq, LANES), jnp.bfloat16),
             pltpu.VMEM((groups, 2 * blocks * GROUP_SIZE, BLOCK), jnp.bfloat16),
             pltpu.VMEM((groups, blocks * GROUP_SIZE, BLOCK), jnp.float32),
-            pltpu.VMEM((BLOCK, seq + LANES), jnp.bfloat16),
+            pltpu.VMEM((groups, LANES, seq + LANES), jnp.bfloat16),
         ],
         compiler_params=pltpu.CompilerParams(vmem_limit_bytes=62 * 2**20),
-    )(holder, recv, reach, taps, skip, bands)
+    )(holder, recv, reach, taps, skip, lags)
 
 
 def exchange_kernel(
-    blocks, axis_peers, holder, loaded, reach, taps, skip, bands, out,
-    recv_q, recv_kv, mixed, xt, yt, toep, gated,
-    kv_send, kv_recv, q_send, q_recv, back_send, back_recv, own_sem,
+    blocks, axis_peers, holder, loaded, reach, taps, skip, filters, out,
+    recv_q, recv_kv, mixed, xt, yt, toep, gated, lags,
+    lag_send, lag_recv, kv_send, kv_recv, q_send, q_recv, back_send, back_recv, own_sem,
 ):
     devices = axis_peers
     me = lax.axis_index("seq")
@@ -154,6 +155,24 @@
 
     def lanes_of(index):
         return pl.ds(pl.multiple_of(index * LANES, LANES), LANES)
+
+    filter_lags = filters.shape[1]
+
+    def lag_rows(index):
+        return filters.at[pl.ds(pl.multiple_of(index * groups, groups), groups), :]
+
+    def lag_place():
+        return lags.at[:, pl.ds(pl.multiple_of(LANES + me * filter_lags, LANES), filter_lags)]
+
+    def lag_copy(k):
+        return pltpu.make_async_remote_copy(
+            src_ref=lag_rows(peer_at(k)),
+            dst_ref=lag_place(),
+            send_sem=lag_send.at[k],
+            recv_sem=lag_recv.at[k],
+            device_id={"seq": peer_at(k)},
+            device_id_type=pl.DeviceIdType.MESH,
+        )
 
     def kv_copy(k):
         return pltpu.make_async_remote_copy(
@@ -204,12 +223,27 @@
     own_q = pltpu.make_async_copy(loaded.at[0:1, :, :, lanes_of(me)], recv_q.at[me], own_sem.at[1])
     own_back = pltpu.make_async_copy(gated.at[rows_of(me)], out.at[:, lanes_of(me)], own_sem.at[2])
 
+    own_lag = pltpu.make_async_copy(lag_rows(me), lag_place(), own_sem.at[3])
+
+    @pl.loop(1, devices)
+    def _(k):
+        lag_copy(k).start()
+
     @pl.loop(1, devices)
     def _(k):
         kv_copy(k).start()
 
+    own_lag.start()
     own_kv.start()
     own_q.start()
+    lags[:, 0:LANES] = jnp.zeros((groups, LANES), jnp.float32)
+    own_lag.wait()
+
+    @pl.loop(1, devices)
+    def _(k):
+        lag_copy(k).wait()
+
+    toeplitz(lags, toep, groups, blocks)
     for g in range(groups):
         xt[g, 0 : blocks * GROUP_SIZE, :] = jnp.zeros((blocks * GROUP_SIZE, BLOCK), xt.dtype)
 
@@ -226,7 +260,7 @@
 
     @pl.loop(0, blocks)
     def _(block):
-        @pl.loop(0, tiles)
+        @pl.loop(0, tiles, unroll=4)
         def _(i):
             row, (k, v) = place_and_filter(
                 holder, recv_kv, reach, taps, (1, 2), 1, block * tiles + i
@@ -235,7 +269,7 @@
 
         to_columns(mixed, xt, groups, block, blocks)
 
-    long_conv(bands, toep, xt, yt, groups, blocks)
+    long_conv(toep, xt, yt, groups, blocks)
 
     own_q.wait()
 
@@ -247,7 +281,7 @@
         for part in range(per_device):
             block = owner * per_device + part
 
-            @pl.loop(0, tiles)
+            @pl.loop(0, tiles, unroll=4)
             def _(i):
                 row, (q,) = place_and_filter(
                     holder, recv_q, reach, taps, (0,), 0, block * tiles + i
@@ -273,7 +307,7 @@
         back_copy(k).wait()
 
 
-def exchange_operator(holder, loaded, reach, taps, skip, bands, devices):
+def exchange_operator(holder, loaded, reach, taps, skip, filters, devices):
     seq = reach.shape[0]
     blocks = seq // BLOCK
     groups = LANES // GROUP_SIZE
@@ -292,21 +326,25 @@
             pltpu.VMEM((seq, LANES), jnp.bfloat16),
             pltpu.VMEM((groups, 2 * blocks * GROUP_SIZE, BLOCK), jnp.bfloat16),
             pltpu.VMEM((groups, blocks * GROUP_SIZE, BLOCK), jnp.float32),
-            pltpu.VMEM((BLOCK, seq + LANES), jnp.bfloat16),
+            pltpu.VMEM((groups, LANES, seq + LANES), jnp.bfloat16),
             pltpu.VMEM((seq, LANES), jnp.bfloat16),
+            pltpu.VMEM((groups, seq + LANES), jnp.float32),
         ]
-        + [dma((devices,))] * 6
-        + [dma((3,))],
+        + [dma((devices,))] * 8
+        + [dma((4,))],
         compiler_params=pltpu.CompilerParams(
             vmem_limit_bytes=60 * 2**20, collective_id=0, has_side_effects=True
         ),
-    )(holder, loaded, reach, taps, skip, bands)
+    )(holder, loaded, reach, taps, skip, filters)
 
 
 def routing(dest_tiles, tile_counts, segments):
     cap = dest_tiles.shape[0]
     marked = jnp.where(jnp.arange(cap, dtype=jnp.int32) < tile_counts[0], dest_tiles, -1)
-    gathered = lax.all_gather(jnp.concatenate([segments, marked]), "seq")
+    devices = lax.axis_size("seq")
+    ints = jnp.concatenate([segments, marked])
+    copies = jnp.broadcast_to(ints, (devices, ints.shape[0]))
+    gathered = lax.all_to_all(copies, "seq", split_axis=0, concat_axis=0, tiled=True)
     docs = gathered[:, : segments.shape[0]].reshape(-1)
     slots = gathered[:, segments.shape[0] :].reshape(-1)
     seq = docs.shape[0]
@@ -321,15 +359,12 @@
     return holder, jnp.broadcast_to(reach.astype(jnp.bfloat16)[:, None], (seq, LANES))
 
 
-def filter_bands(long_filters, devices, groups):
-    count, lags = long_filters.shape
+def whole_filters(long_filters, devices, groups):
+    count = long_filters.shape[0]
     if count < devices * groups:
         long_filters = jnp.repeat(long_filters, devices * groups // count, axis=0)
     mine = lax.all_to_all(long_filters, "seq", split_axis=0, concat_axis=1, tiled=True)
-    seq = mine.shape[1]
-    padded = jnp.pad(mine, ((0, 0), (LANES, 0)))
-    shifted = [padded] + [jnp.pad(padded, ((0, 0), (s, 0)))[:, : seq + LANES] for s in range(1, 16)]
-    return jnp.stack(shifted, axis=1)
+    return jnp.pad(mine.astype(jnp.float32), ((0, 0), (LANES, 0)))
 
 
 def local(
@@ -345,19 +380,20 @@
     me = lax.axis_index("seq")
     pad = LANES - width
     holder, reach = routing(dest_tiles, tile_counts, segments)
-    bands = filter_bands(long_filters, devices, groups)
     taps = lax.dynamic_slice_in_dim(short_filters, me * width, width, 2)
     taps = jnp.pad(taps, ((0, 0), (0, 1), (0, pad)))
     skip = jnp.pad(lax.dynamic_slice_in_dim(skip_gain, me * width, width, 0), (0, pad))[None, :]
     if width == LANES:
+        filters = long_filters.astype(jnp.float32)
         tiled = loaded.reshape(3, cap, TILE, chans_here)
-        arrived = exchange_operator(holder, tiled, reach, taps, skip, bands, devices)
+        arrived = exchange_operator(holder, tiled, reach, taps, skip, filters, devices)
     else:
+        lags = whole_filters(long_filters, devices, groups)
         sliced = jnp.transpose(loaded.reshape(3, rows, devices, width), (2, 0, 1, 3))
         recv = lax.all_to_all(sliced, "seq", split_axis=0, concat_axis=0, tiled=True)
         recv = jnp.pad(recv, ((0, 0), (0, 0), (0, 0), (0, pad)))
         recv = recv.reshape(devices, 3, cap, TILE, LANES)
-        gated = operator(holder, recv, reach, taps, skip, bands, groups)[:, :width]
+        gated = operator(holder, recv, reach, taps, skip, lags, groups)[:, :width]
         seq_rows = gated.shape[0] // devices
         back = lax.all_to_all(
             gated.reshape(devices, seq_rows, width), "seq", split_axis=0, concat_axis=0, tiled=True

time: 457 us -> 371 us (0.81)
  blocking collectives: 48.2 us -> 3.8 us
  Pallas kernels: 365 us -> 343 us
  local copies, waits for them, and re-layouts: 26 us -> 4.91 us
    unnamed x1 -> x0, blocking collectives: 44.4 us -> none
    pallas_call x1, Pallas kernels: 365 us -> 343 us  [exchange_operator(): pl.pallas_call(functools.partial(exchange_kernel, blocks, devices), out_s...]
    another operation x18 -> x0, local copies, waits for them, and re-layouts: 20.4 us -> none  [filter_bands(): return jnp.stack(shifted, axis=1)]
  transfers between devices with their start and end apart: 1 -> 1, of which waited for: 0 -> 1; matrix products, arithmetic and copies ran while one was open for 1% -> 1% of each run, Pallas kernels for 0% -> 0%
where the time goes in v3:
time: 371 us; the launch traced here: 370 us
  Pallas kernels  343 us (92%)
  other arithmetic  9.89 us (3%)
  starting transfers between devices  6.55 us (2%)
  local copies, waits for them, and re-layouts  4.91 us (1%)
  blocking collectives  3.8 us (1%)
    pallas_call x1, Pallas kernels, exchange_operator(): pl.pallas_call(functools.partial(exchange_kernel, blocks, devices), out_s...  343 us
  transfers between devices with their start and end apart: 1, of which 1 were waited for; matrix products, arithmetic and copies ran while one was open for 1% of the time, Pallas kernels for 0%

profile of v3, /device:TPU:11, one launch (start us, length us, event | category | flops | bytes accessed | tf_op | source)
XLA Modules:
  0.0 369.9 jit_solution(10809603286396678773)
XLA Ops:
  0.0 0.0 copy-start
  0.7 0.7 compare_select_fusion.3
  1.4 0.7 pad_add_fusion
  2.0 0.6 broadcast_in_dim.33
  2.7 6.6 %all-to-all-start = ((s32[16,1,544]{2,1,0:T(1,128)}), s32[16,1,544]{2,1,0:T(1,128)S(1)}, u32[]{:S(2)}, u32[]{:S(2)}) async-start(s32[16,1,544]{2,1,0:T(1,128)} %broadcast_in_dim.33), calls=%async_computation | async-start | bytes 81920 | tf_op jit(solution)/shard_map/all_to_all | solution.py:347
  9.2 1.7 convert_element_type.11.filters
  10.9 0.0 copy-done
  10.9 0.6 pad.58.taps
  11.5 1.3 dynamic-slice_bitcast_fusion.skip
  12.8 0.6 all-to-all-done
  13.5 0.1 slice_compare_fusion.3
  13.5 0.1 slice_compare_fusion
  13.6 0.1 slice_compare_fusion.4
  13.7 0.1 slice_compare_fusion.2
  13.8 0.1 slice_compare_fusion.5
  13.9 0.1 slice_compare_fusion.1
  14.0 0.1 eq.35
  14.0 0.1 select_reduce_fusion
  14.2 0.6 pad_add_fusion.1.holder
  14.8 0.1 add_convert_fusion
  14.9 2.2 broadcast_in_dim.36.reach
  17.1 0.0 copy-start.1
  17.1 343.4 %shard_map.82 = bf16[512,2048]{1,0:T(8,128)(2,1)} custom-call(s32[2,256]{1,0:T(2,128)} %pad_add_fusion.1.holder, bf16[3,32,32,2048]{3,2,1,0:T(8,128)(2,1)} %bitcast.12, bf16[8192,128]{1,0:T(8,128)(2,1)} %broadcast_in_dim.36.reach, f32[3,8,128]{2,1,0:T(8,128)} %pad.58.taps, f32[1,128]{1,0:T(1,128)} %dynamic-slice_bitcast_fusion.skip, ...), custom_call_target="tpu_custom_call" | custom-call | tf_op jit(solution)/shard_map/pallas_call | solution.py:318
  360.6 2.1 fusion
  362.6 3.8 %psum.7 = f32[512]{0:T(512)S(1)} all-reduce(f32[512]{0:T(512)S(1)} %fusion), channel_id=1, replica_groups=mesh['seq'=16,'chan'=2] {'chan'}, use_global_device_ids=true, to_apply=%region_2.3 | all-reduce | flops 512 | bytes 4096 | tf_op jit(solution)/shard_map/psum | solution.py:403
  366.5 0.0 copy-done.1
  366.5 3.5 fusion.2
  (8 shorter events, 0.1 us)
Async XLA Ops:
  0.0 10.9 %copy-start = (f32[3,7,2048]{2,1,0:T(8,128)S(1)}, f32[3,7,2048]{2,1,0:T(8,128)}, u32[]{:S(2)}) copy-start(f32[3,7,2048]{2,1,0:T(8,128)} %param.12) | copy-start | bytes 516100
  2.7 10.7 %all-to-all-start = ((s32[16,1,544]{2,1,0:T(1,128)}), s32[16,1,544]{2,1,0:T(1,128)S(1)}, u32[]{:S(2)}, u32[]{:S(2)}) async-start(s32[16,1,544]{2,1,0:T(1,128)} %broadcast_in_dim.33), calls=%async_computation | async-start | bytes 81920 | tf_op jit(solution)/shard_map/all_to_all | solution.py:347
  17.1 349.3 %copy-start.1 = (f32[2048]{0:T(1024)S(1)}, f32[2048]{0:T(1024)}, u32[]{:S(2)}) copy-start(f32[2048]{0:T(1024)} %param.15) | copy-start | bytes 24580

commit v4 on v3

--- a/solution.py
+++ b/solution.py
@@ -151,7 +151,8 @@
     per_device = seq_rows // BLOCK
 
     def peer_at(k):
-        return lax.rem(me + k, devices)
+        distance = devices // 2 + (k // 2) * (2 * (k % 2) - 1)
+        return lax.rem(me + distance, devices)
 
     def lanes_of(index):
         return pl.ds(pl.multiple_of(index * LANES, LANES), LANES)

time: 371 us -> 362 us (0.976)
  Pallas kernels: 343 us -> 334 us
    pallas_call x1, Pallas kernels: 343 us -> 334 us  [exchange_operator(): pl.pallas_call(functools.partial(exchange_kernel, blocks, devices), out_s...]
where the time goes in v4:
time: 362 us; the launch traced here: 361 us
  Pallas kernels  334 us (92%)
  other arithmetic  9.89 us (3%)
  starting transfers between devices  6.55 us (2%)
  local copies, waits for them, and re-layouts  4.91 us (1%)
  blocking collectives  4.12 us (1%)
    pallas_call x1, Pallas kernels, exchange_operator(): pl.pallas_call(functools.partial(exchange_kernel, blocks, devices), out_s...  334 us
  transfers between devices with their start and end apart: 1, of which 1 were waited for; matrix products, arithmetic and copies ran while one was open for 1% of the time, Pallas kernels for 0%

profile of v4, /device:TPU:11, one launch (start us, length us, event | category | flops | bytes accessed | tf_op | source)
XLA Modules:
  0.0 360.7 jit_solution(12641884114942548302)
XLA Ops:
  0.0 0.0 copy-start
  0.7 0.7 compare_select_fusion.3
  1.4 0.7 pad_add_fusion
  2.0 0.6 broadcast_in_dim.33
  2.7 6.6 %all-to-all-start = ((s32[16,1,544]{2,1,0:T(1,128)}), s32[16,1,544]{2,1,0:T(1,128)S(1)}, u32[]{:S(2)}, u32[]{:S(2)}) async-start(s32[16,1,544]{2,1,0:T(1,128)} %broadcast_in_dim.33), calls=%async_computation | async-start | bytes 81920 | tf_op jit(solution)/shard_map/all_to_all | solution.py:348
  9.2 1.7 convert_element_type.11.filters
  10.9 0.0 copy-done
  10.9 0.6 pad.58.taps
  11.5 1.3 dynamic-slice_bitcast_fusion.skip
  12.8 0.6 all-to-all-done
  13.5 0.1 slice_compare_fusion.3
  13.5 0.1 slice_compare_fusion
  13.6 0.1 slice_compare_fusion.4
  13.7 0.1 slice_compare_fusion.2
  13.8 0.1 slice_compare_fusion.5
  13.9 0.1 slice_compare_fusion.1
  14.0 0.1 eq.35
  14.0 0.1 select_reduce_fusion
  14.2 0.6 pad_add_fusion.1.holder
  14.8 0.1 add_convert_fusion
  14.9 2.2 broadcast_in_dim.36.reach
  17.1 0.0 copy-start.1
  17.1 333.9 %shard_map.82 = bf16[512,2048]{1,0:T(8,128)(2,1)} custom-call(s32[2,256]{1,0:T(2,128)} %pad_add_fusion.1.holder, bf16[3,32,32,2048]{3,2,1,0:T(8,128)(2,1)} %bitcast.12, bf16[8192,128]{1,0:T(8,128)(2,1)} %broadcast_in_dim.36.reach, f32[3,8,128]{2,1,0:T(8,128)} %pad.58.taps, f32[1,128]{1,0:T(1,128)} %dynamic-slice_bitcast_fusion.skip, ...), custom_call_target="tpu_custom_call" | custom-call | tf_op jit(solution)/shard_map/pallas_call | solution.py:319
  351.1 2.1 fusion
  353.2 4.1 %psum.7 = f32[512]{0:T(512)S(1)} all-reduce(f32[512]{0:T(512)S(1)} %fusion), channel_id=1, replica_groups=mesh['seq'=16,'chan'=2] {'chan'}, use_global_device_ids=true, to_apply=%region_2.3 | all-reduce | flops 512 | bytes 4096 | tf_op jit(solution)/shard_map/psum | solution.py:404
  357.3 0.0 copy-done.1
  357.3 3.5 fusion.2
  (8 shorter events, 0.1 us)
Async XLA Ops:
  0.0 10.9 %copy-start = (f32[3,7,2048]{2,1,0:T(8,128)S(1)}, f32[3,7,2048]{2,1,0:T(8,128)}, u32[]{:S(2)}) copy-start(f32[3,7,2048]{2,1,0:T(8,128)} %param.12) | copy-start | bytes 516100
  2.7 10.7 %all-to-all-start = ((s32[16,1,544]{2,1,0:T(1,128)}), s32[16,1,544]{2,1,0:T(1,128)S(1)}, u32[]{:S(2)}, u32[]{:S(2)}) async-start(s32[16,1,544]{2,1,0:T(1,128)} %broadcast_in_dim.33), calls=%async_computation | async-start | bytes 81920 | tf_op jit(solution)/shard_map/all_to_all | solution.py:348
  17.1 340.1 %copy-start.1 = (f32[2048]{0:T(1024)S(1)}, f32[2048]{0:T(1024)}, u32[]{:S(2)}) copy-start(f32[2048]{0:T(1024)} %param.15) | copy-start | bytes 24580
